TPU v7x, 256 devices: a whole 4x4x8 slice. The times are simulated.
256 devices in a mesh: chan: 32 (over z, y_hi, core), tile: 8 (over x, y_lo).
Axes of the slice: x: 4, y: 4 (y_hi: 2, y_lo: 2; y = y_hi * 2 + y_lo), z: 8, core: 2. Of those that a mesh axis runs over, the one named last changes fastest.
Arguments:
- voltages: int32 [2, 512, 323584], P(None, ('tile', 'chan')), may hold values from -128 to 127
- filter_taps: float32 [16, 4096], replicated, may hold values from -0.02 to 0.02
Outputs:
- visibilities: bfloat16 [2048, 512, 512], P(('chan', 'tile'))
All inputs are finite; a program needn't handle non-finite values.
Results may differ from a plain program's by a relative error of at most 0.0055.
Values may be sent and summed in bfloat16 or wider, within the bound.
A program may use at most 64 MiB of HBM per device.

v0:
```python
import functools
import math

import jax
import jax.numpy as jnp
import ml_dtypes
import numpy as np
from jax import lax
from jax.experimental import pallas as pl
from jax.experimental.pallas import tpu as pltpu
from jax.sharding import PartitionSpec as P

MESH = pl.DeviceIdType.MESH
NFFT, TAPS, SPEC, KEEP = 4096, 16, 64, 2048
FRAMES = SPEC + TAPS - 1
LANES = 128
R1 = NFFT // LANES
C2 = KEEP // R1
SB = 16
BLOCKS = SPEC // SB
FIRST = SB + TAPS - 1
HALF = TAPS // 2
NT = (((1,), (1,)), ((), ()))


def split(values):
    high = values.astype(ml_dtypes.bfloat16)
    low = (values - high.astype(np.float64)).astype(ml_dtypes.bfloat16)
    return high, low


@functools.cache
def first_table():
    c1, j = np.meshgrid(np.arange(R1), np.arange(R1), indexing="ij")
    angle = 2 * math.pi * ((c1 * j) % R1) / R1
    cos, sin = np.cos(angle), np.sin(angle)
    unit = np.concatenate([np.concatenate([cos, sin], 1), np.concatenate([-sin, cos], 1)], 0)
    return np.concatenate(split(np.kron(np.eye(4), unit)), 0)


@functools.cache
def second_table():
    chan = np.arange(R1)[:, None, None] + R1 * np.arange(C2)[None, :, None]
    angle = 2 * math.pi * ((chan * np.arange(LANES)) % NFFT) / NFFT
    full = np.concatenate([np.cos(angle), -np.sin(angle)], 2) / math.sqrt(NFFT)
    return np.concatenate(split(full), 1)


Z_ORDER = (4, 3, 5, 2, 6, 1, 7, 0)


def chan_table():
    chan = lax.axis_index("chan")
    z, high, core = lax.div(chan, 4), lax.rem(lax.div(chan, 2), 2), lax.rem(chan, 2)
    z_part = [lax.rem(z + dz, 8) * 4 for dz in range(8)]
    y_part = [high * 2, 2 - high * 2]
    c_part = [core, 1 - core]
    return chan, {(dz, dh, dc): z_part[dz] + (y_part[dh] + c_part[dc]) for dz in range(8) for dh in range(2) for dc in range(2)}


def signal(sem, chan, tile):
    pl.semaphore_signal(sem, inc=1, device_id={"chan": chan, "tile": tile}, device_id_type=MESH)


def channelize(v_hbm, h_hbm, d_hbm, w_hbm, out_hbm, vbuf, hraw, hbuf, dbuf, wbuf, xs, af, sbuf, msg, got, ordered, vsem, csem, osem, send, recv, ready):
    barrier = pltpu.get_barrier_semaphore()
    chan, chan_at = chan_table()
    tile = lax.axis_index("tile")
    tile_at = [lax.rem(tile + step, 8) for step in range(8)]
    me = tile * 32 + chan

    def frames_in(part, chunk):
        where = pl.ds(0, FIRST) if isinstance(chunk, int) and chunk == 0 else pl.ds(chunk * SB + TAPS - 1, SB)
        return pltpu.make_async_copy(v_hbm.at[part, where], vbuf.at[part, where], vsem.at[part, chunk])

    taps_in = pltpu.make_async_copy(h_hbm, hraw, csem.at[0])
    first_in = pltpu.make_async_copy(d_hbm, dbuf, csem.at[1])
    second_in = pltpu.make_async_copy(w_hbm, wbuf, csem.at[2])
    taps_in.start()
    frames_in(0, 0).start()
    frames_in(1, 0).start()
    first_in.start()
    for chunk in range(1, BLOCKS):
        for part in range(2):
            frames_in(part, chunk).start()
    second_in.start()

    for dz in Z_ORDER:
        for dh in range(2):
            for dc in range(2):
                if dz or dh or dc:
                    signal(barrier, chan_at[dz, dh, dc], tile)
    for step in range(1, 8):
        signal(barrier, chan, tile_at[step])

    taps_in.wait()
    for block in range(4):
        for i in range(HALF):
            even, odd = [
                hraw[pl.ds((tap // 8) * 256 + block * 64 + tap % 8, 8, stride=8), :] for tap in (2 * i, 2 * i + 1)
            ]
            rows = slice(block * 8, block * 8 + 8)
            hbuf[i, rows, :] = even
            hbuf[HALF + i, rows, :] = odd
            hbuf[2 * HALF + i, rows, :] = even + odd

    def filter_rows(sig, part, block, base):
        rows = slice(block * 8, block * 8 + 8)
        here = pl.ds(block * 16 + sig, 8, stride=2)
        window = vbuf[part, pl.ds(base, FIRST - 1), here, :].astype(jnp.float32).reshape(FIRST // 2, 2, 8, LANES)
        last = vbuf[part, pl.ds(base + FIRST - 1, 1), here, :].astype(jnp.float32)
        even, odd = window[:, 0], window[:, 1]
        ahead = jnp.concatenate([even[1:], last], axis=0)

        def short(which, values):
            total = hbuf[which * HALF, rows, :][None] * values[0 : SB // 2]
            for i in range(1, HALF):
                total = total + hbuf[which * HALF + i, rows, :][None] * values[i : i + SB // 2]
            return total

        shared = short(2, odd)
        first = short(0, even - odd) + shared
        second = short(1, ahead - odd) + shared
        return jnp.stack([first, second], axis=1).reshape(SB, 8, LANES)

    def filter_block(sig, number):
        base = number * SB
        for part in range(2):
            for pair in range(2):
                both = jnp.concatenate([filter_rows(sig, part, 2 * pair + i, base) for i in range(2)], axis=1)
                xs[:, part * 32 + pair * 16 : part * 32 + pair * 16 + 16, :] = both.astype(jnp.bfloat16)
        for half in range(SB // 8):
            right = jnp.concatenate([xs[half * 8 + 4 * q : half * 8 + 4 * q + 4].reshape(256, LANES) for q in range(2)], axis=1)
            out = jnp.dot(dbuf[...], right, preferred_element_type=jnp.float32)
            out = out[:256] + out[256:]
            for q in range(2):
                af[pl.ds(pl.multiple_of((base + half * 8 + 4 * q) * 64, 256), 256), :] = out[:, q * 128 : (q + 1) * 128]

    def send_to(sig, turn, group, to_chan, half):
        pltpu.make_async_remote_copy(
            src_ref=msg.at[(sig * 4 + turn) * C2 + half + 2 * to_chan],
            dst_ref=got.at[sig * 256 + me],
            send_sem=send,
            recv_sem=recv.at[sig * 4 + turn],
            device_id={"chan": to_chan, "tile": half * 4 + group},
            device_id_type=MESH,
        ).start()

    def group_step(sig, turn):
        group = lax.rem(tile + turn, 4)
        for k in range(8):
            c1 = group * 8 + k
            real = af[pl.ds(c1, SPEC, stride=64), :]
            imag = af[pl.ds(R1 + c1, SPEC, stride=64), :]
            right = jnp.concatenate(
                [jnp.concatenate([real, -imag], axis=1), jnp.concatenate([imag, real], axis=1)], axis=0
            ).astype(jnp.bfloat16)
            out = lax.dot_general(wbuf[c1], right, NT, preferred_element_type=jnp.float32)
            sbuf[k * C2 : (k + 1) * C2, :] = out[:C2] + out[C2:]
        for c2 in range(C2):
            msg[(sig * 4 + turn) * C2 + c2] = sbuf[pl.ds(c2, 8, stride=C2), :].astype(jnp.bfloat16)
        halves = [lax.div(tile, 4), 1 - lax.div(tile, 4)]
        for dx in range(2):
            if dx and sig == 0:

                @pl.when(turn == 0)
                def _():
                    pl.semaphore_wait(ready, 7)

            for dh in range(2):
                for dz in Z_ORDER:
                    for dc in range(2):
                        to = functools.partial(send_to, sig, turn, group, chan_at[dz, dh, dc], halves[dx])
                        if dx or dh or dz or dc:
                            to()
                        else:
                            pl.when(turn != 0)(to)

    for sig in range(2):

        def filter_step(number, carry):
            if sig == 0:

                @pl.when(number > 0)
                def _():
                    frames_in(0, number).wait()
                    frames_in(1, number).wait()

            filter_block(sig, number)
            return carry

        def send_step(turn, carry):
            group_step(sig, turn)
            return carry

        if sig == 0:
            frames_in(0, 0).wait()
            frames_in(1, 0).wait()
            first_in.wait()
        lax.fori_loop(0, BLOCKS, filter_step, 0)
        if sig == 0:
            pl.semaphore_wait(barrier, 38)
            for step in range(1, 8):
                signal(ready, chan, tile_at[step])
            second_in.wait()
        lax.fori_loop(0, 4, send_step, 0)
        got[sig * 256 + me] = msg[sig * 256 + 2 * chan + lax.div(tile, 4)]

    to = lax.broadcasted_iota(jnp.int32, (256, 256), 0)
    come = lax.broadcasted_iota(jnp.int32, (256, 256), 1)
    sort = (to == (come % 8) * 32 + (come // 8 % 16) * 2 + come // 128).astype(jnp.bfloat16)

    def out_copy(from_tile, slot):
        where = pl.ds(pl.multiple_of(from_tile * 64, 64), 64)
        return pltpu.make_async_copy(ordered.at[:, where], out_hbm.at[:, where], osem.at[slot])

    for turn in range(4):
        for sig in range(2):
            count = pl.ds(0, 64 if turn else 63)
            pltpu.make_async_copy(msg.at[count], got.at[count], recv.at[sig * 4 + turn]).wait()
        group = lax.rem(tile + 4 - turn, 4)
        for half in range(2):
            from_tile = half * 4 + group
            right = jnp.concatenate(
                [
                    jnp.concatenate(
                        [got[pl.ds(sig * 256 + from_tile * 32 + 16 * q, 16)].reshape(128, LANES) for sig in range(2)], axis=0
                    )
                    for q in range(2)
                ],
                axis=1,
            )
            rows = jnp.dot(sort, right, preferred_element_type=jnp.float32).astype(jnp.bfloat16)
            for q in range(2):
                here = pl.ds(pl.multiple_of(from_tile * 64 + 32 * q, 32), 32)
                ordered[:, here, :] = rows[:, q * 128 : (q + 1) * 128].reshape(8, 32, LANES)
            out_copy(from_tile, turn * 2 + half).start()
    for turn in range(4):
        for half in range(2):
            out_copy(half * 4 + lax.rem(tile + 4 - turn, 4), turn * 2 + half).wait()
    everything = pl.ds(0, 510)
    pltpu.make_async_copy(msg.at[everything], got.at[everything], send).wait()


def correlate(x_hbm, out_hbm, x, out, isem, osem):
    ins = [pltpu.make_async_copy(x_hbm.at[k], x.at[k], isem.at[k]) for k in range(8)]
    outs = [pltpu.make_async_copy(out.at[k], out_hbm.at[k], osem.at[k]) for k in range(8)]
    for copy in ins:
        copy.start()
    upper = lax.broadcasted_iota(jnp.int32, (256, 256), 0) <= lax.broadcasted_iota(jnp.int32, (256, 256), 1)
    for k in range(8):
        ins[k].wait()
        here = x[k]
        wide = here.astype(jnp.float32)
        turned = jnp.concatenate([wide[:, SPEC:], -wide[:, :SPEC]], axis=1).astype(jnp.bfloat16)

        def product(left, lo, hi):
            return lax.dot_general(
                left[lo * 256 : lo * 256 + 256], here[hi * 256 : hi * 256 + 256], NT, preferred_element_type=jnp.float32
            )

        for lo in range(2):
            for hi in range(2):
                if lo < hi:
                    block = product(here, lo, hi)
                elif lo > hi:
                    block = product(turned, lo, hi)
                else:
                    block = jnp.where(upper, product(here, lo, hi), product(turned, lo, hi))
                out[k, lo * 256 : lo * 256 + 256, hi * 256 : hi * 256 + 256] = (block * (1.0 / SPEC)).astype(jnp.bfloat16)
        outs[k].start()
    for copy in outs:
        copy.wait()


def per_device(voltages, filter_taps):
    rows = NFFT // LANES
    frames = voltages.reshape(2, 2, FRAMES * rows, LANES).transpose(0, 2, 1, 3).reshape(2, FRAMES, 2 * rows, LANES)
    taps = filter_taps.reshape(2, 8, rows, LANES).transpose(0, 2, 1, 3).reshape(2 * rows * 8, LANES)
    first, second = first_table(), second_table()
    hbm = pl.BlockSpec(memory_space=pl.ANY)
    dma = pltpu.SemaphoreType.DMA
    ordered = pl.pallas_call(
        channelize,
        name="channelize",
        out_shape=jax.ShapeDtypeStruct((8, 512, LANES), jnp.bfloat16),
        in_specs=[hbm] * 4,
        out_specs=hbm,
        scratch_shapes=[
            pltpu.VMEM((2, FRAMES, 2 * rows, LANES), jnp.int32),
            pltpu.VMEM(taps.shape, jnp.float32),
            pltpu.VMEM((3 * HALF, rows, LANES), jnp.float32),
            pltpu.VMEM(first.shape, jnp.bfloat16),
            pltpu.VMEM(second.shape, jnp.bfloat16),
            pltpu.VMEM((SB, 2 * rows, LANES), jnp.bfloat16),
            pltpu.VMEM((SPEC * 64, LANES), jnp.float32),
            pltpu.VMEM((8 * C2, LANES), jnp.float32),
            pltpu.VMEM((512, 8, LANES), jnp.bfloat16),
            pltpu.VMEM((512, 8, LANES), jnp.bfloat16),
            pltpu.VMEM((8, 512, LANES), jnp.bfloat16),
            dma((2, BLOCKS)),
            dma((3,)),
            dma((8,)),
            dma,
            dma((8,)),
            pltpu.SemaphoreType.REGULAR,
        ],
        compiler_params=pltpu.CompilerParams(collective_id=0, has_side_effects=True, vmem_limit_bytes=60 << 20),
    )(frames, taps, jnp.asarray(first), jnp.asarray(second))
    return pl.pallas_call(
        correlate,
        name="correlate",
        out_shape=jax.ShapeDtypeStruct((8, 512, 512), jnp.bfloat16),
        in_specs=[hbm],
        out_specs=hbm,
        scratch_shapes=[
            pltpu.VMEM((8, 512, LANES), jnp.bfloat16),
            pltpu.VMEM((8, 512, 512), jnp.bfloat16),
            dma((8,)),
            dma((8,)),
        ],
        compiler_params=pltpu.CompilerParams(vmem_limit_bytes=60 << 20),
    )(ordered)


def solution(mesh):
    return jax.shard_map(
        per_device,
        mesh=mesh,
        in_specs=(P(None, ("tile", "chan"), None), P()),
        out_specs=P(("chan", "tile"), None, None),
        check_vma=False,
    )
```

profile of v0, /device:TPU:1, one launch (start us, length us, event | category | flops | bytes accessed | tf_op | source)
XLA Modules:
  0.0 48.8 jit_solution(10818683593987844363)
XLA Ops:
  0.0 43.7 %channelize.1.x_hbm = bf16[8,512,128]{2,1,0:T(8,128)(2,1)} custom-call(s32[2,79,64,128]{3,2,1,0:T(8,128)} %bitcast.10, f32[512,128]{1,0:T(8,128)} %bitcast.11, bf16[512,256]{1,0:T(8,128)(2,1)} %constant.4.clone.d_hbm, bf16[32,128,256]{2,1,0:T(8,128)(2,1)} %constant.5.clone.w_hbm), custom_call_target="tpu_custom_call" | custom-call | tf_op jit(solution)/shard_map/channelize/pallas_call | solution.py:283
  43.7 5.1 %correlate.1 = bf16[8,512,512]{2,1,0:T(8,128)(2,1)} custom-call(bf16[8,512,128]{2,1,0:T(8,128)(2,1)} %channelize.1.x_hbm), custom_call_target="tpu_custom_call" | custom-call | tf_op jit(solution)/shard_map/correlate/pallas_call | solution.py:310
where the time goes:
time: 48.9 us; the launch traced here: 48.8 us
  Pallas kernels  48.8 us (100%)
    pallas_call x1, Pallas kernels, per_device(): pl.pallas_call(channelize, name='channelize', out_shape=jax.ShapeDtypeStr...  43.7 us
    pallas_call x1, Pallas kernels, per_device(): pl.pallas_call(correlate, name='correlate', out_shape=jax.ShapeDtypeStruc...  5.1 us

commit v1 on v0

--- a/solution.py
+++ b/solution.py
@@ -35,14 +35,14 @@
     angle = 2 * math.pi * ((c1 * j) % R1) / R1
     cos, sin = np.cos(angle), np.sin(angle)
     unit = np.concatenate([np.concatenate([cos, sin], 1), np.concatenate([-sin, cos], 1)], 0)
-    return np.concatenate(split(np.kron(np.eye(4), unit)), 0)
+    return np.concatenate(split(np.kron(np.eye(2), unit)), 1)
 
 
 @functools.cache
 def second_table():
     chan = np.arange(R1)[:, None, None] + R1 * np.arange(C2)[None, :, None]
     angle = 2 * math.pi * ((chan * np.arange(LANES)) % NFFT) / NFFT
-    full = np.concatenate([np.cos(angle), -np.sin(angle)], 2) / math.sqrt(NFFT)
+    full = np.concatenate([np.cos(angle), -np.sin(angle)], 2) / (math.sqrt(NFFT) * math.sqrt(SPEC))
     return np.concatenate(split(full), 1)
 
 
@@ -62,7 +62,7 @@
     pl.semaphore_signal(sem, inc=1, device_id={"chan": chan, "tile": tile}, device_id_type=MESH)
 
 
-def channelize(v_hbm, h_hbm, d_hbm, w_hbm, out_hbm, vbuf, hraw, hbuf, dbuf, wbuf, xs, af, sbuf, msg, got, ordered, vsem, csem, osem, send, recv, ready):
+def channelize(v_hbm, hraw, t_hbm, ordered, vbuf, hbuf, dbuf, wbuf, xs, af, sbuf, msg, got, vsem, csem, send, recv, ready):
     barrier = pltpu.get_barrier_semaphore()
     chan, chan_at = chan_table()
     tile = lax.axis_index("tile")
@@ -73,10 +73,8 @@
         where = pl.ds(0, FIRST) if isinstance(chunk, int) and chunk == 0 else pl.ds(chunk * SB + TAPS - 1, SB)
         return pltpu.make_async_copy(v_hbm.at[part, where], vbuf.at[part, where], vsem.at[part, chunk])
 
-    taps_in = pltpu.make_async_copy(h_hbm, hraw, csem.at[0])
-    first_in = pltpu.make_async_copy(d_hbm, dbuf, csem.at[1])
-    second_in = pltpu.make_async_copy(w_hbm, wbuf, csem.at[2])
-    taps_in.start()
+    first_in = pltpu.make_async_copy(t_hbm.at[R1], dbuf, csem.at[0])
+    second_in = pltpu.make_async_copy(t_hbm.at[pl.ds(0, R1)], wbuf, csem.at[1])
     frames_in(0, 0).start()
     frames_in(1, 0).start()
     first_in.start()
@@ -86,14 +84,14 @@
     second_in.start()
 
     for dz in Z_ORDER:
-        for dh in range(2):
-            for dc in range(2):
-                if dz or dh or dc:
-                    signal(barrier, chan_at[dz, dh, dc], tile)
-    for step in range(1, 8):
-        signal(barrier, chan, tile_at[step])
-
-    taps_in.wait()
+        for dx in range(2):
+            for dh in range(2):
+                for dc in range(2):
+                    if dz or dx or dh or dc:
+                        signal(barrier, chan_at[dz, dh, dc], tile_at[4 * dx])
+    for turn in range(1, 4):
+        signal(barrier, chan, tile_at[turn])
+
     for block in range(4):
         for i in range(HALF):
             even, odd = [
@@ -129,12 +127,12 @@
             for pair in range(2):
                 both = jnp.concatenate([filter_rows(sig, part, 2 * pair + i, base) for i in range(2)], axis=1)
                 xs[:, part * 32 + pair * 16 : part * 32 + pair * 16 + 16, :] = both.astype(jnp.bfloat16)
-        for half in range(SB // 8):
-            right = jnp.concatenate([xs[half * 8 + 4 * q : half * 8 + 4 * q + 4].reshape(256, LANES) for q in range(2)], axis=1)
+        for quad in range(SB // 4):
+            pairs = [xs[quad * 4 + 2 * q : quad * 4 + 2 * q + 2].reshape(128, LANES) for q in range(2)]
+            right = jnp.concatenate([jnp.concatenate([pair, pair], axis=0) for pair in pairs], axis=1)
             out = jnp.dot(dbuf[...], right, preferred_element_type=jnp.float32)
-            out = out[:256] + out[256:]
             for q in range(2):
-                af[pl.ds(pl.multiple_of((base + half * 8 + 4 * q) * 64, 256), 256), :] = out[:, q * 128 : (q + 1) * 128]
+                af[pl.ds(pl.multiple_of((base + quad * 4 + 2 * q) * 64, 128), 128), :] = out[:, q * 128 : (q + 1) * 128]
 
     def send_to(sig, turn, group, to_chan, half):
         pltpu.make_async_remote_copy(
@@ -159,14 +157,14 @@
             sbuf[k * C2 : (k + 1) * C2, :] = out[:C2] + out[C2:]
         for c2 in range(C2):
             msg[(sig * 4 + turn) * C2 + c2] = sbuf[pl.ds(c2, 8, stride=C2), :].astype(jnp.bfloat16)
+        if sig == 0:
+
+            @pl.when(turn > 0)
+            def _():
+                pl.semaphore_wait(ready.at[turn], 1)
+
         halves = [lax.div(tile, 4), 1 - lax.div(tile, 4)]
         for dx in range(2):
-            if dx and sig == 0:
-
-                @pl.when(turn == 0)
-                def _():
-                    pl.semaphore_wait(ready, 7)
-
             for dh in range(2):
                 for dz in Z_ORDER:
                     for dc in range(2):
@@ -199,9 +197,9 @@
             first_in.wait()
         lax.fori_loop(0, BLOCKS, filter_step, 0)
         if sig == 0:
-            pl.semaphore_wait(barrier, 38)
-            for step in range(1, 8):
-                signal(ready, chan, tile_at[step])
+            pl.semaphore_wait(barrier, 66)
+            for turn in range(1, 4):
+                signal(ready.at[turn], chan, tile_at[8 - turn])
             second_in.wait()
         lax.fori_loop(0, 4, send_step, 0)
         got[sig * 256 + me] = msg[sig * 256 + 2 * chan + lax.div(tile, 4)]
@@ -209,10 +207,6 @@
     to = lax.broadcasted_iota(jnp.int32, (256, 256), 0)
     come = lax.broadcasted_iota(jnp.int32, (256, 256), 1)
     sort = (to == (come % 8) * 32 + (come // 8 % 16) * 2 + come // 128).astype(jnp.bfloat16)
-
-    def out_copy(from_tile, slot):
-        where = pl.ds(pl.multiple_of(from_tile * 64, 64), 64)
-        return pltpu.make_async_copy(ordered.at[:, where], out_hbm.at[:, where], osem.at[slot])
 
     for turn in range(4):
         for sig in range(2):
@@ -230,44 +224,34 @@
                 ],
                 axis=1,
             )
-            rows = jnp.dot(sort, right, preferred_element_type=jnp.float32).astype(jnp.bfloat16)
+            rows = jnp.dot(sort, right, preferred_element_type=jnp.float32)
             for q in range(2):
                 here = pl.ds(pl.multiple_of(from_tile * 64 + 32 * q, 32), 32)
-                ordered[:, here, :] = rows[:, q * 128 : (q + 1) * 128].reshape(8, 32, LANES)
-            out_copy(from_tile, turn * 2 + half).start()
-    for turn in range(4):
-        for half in range(2):
-            out_copy(half * 4 + lax.rem(tile + 4 - turn, 4), turn * 2 + half).wait()
+                part = rows[:, q * 128 : (q + 1) * 128]
+                ordered[:, here, :] = part.astype(jnp.bfloat16).reshape(8, 32, LANES)
     everything = pl.ds(0, 510)
     pltpu.make_async_copy(msg.at[everything], got.at[everything], send).wait()
 
 
-def correlate(x_hbm, out_hbm, x, out, isem, osem):
-    ins = [pltpu.make_async_copy(x_hbm.at[k], x.at[k], isem.at[k]) for k in range(8)]
+def correlate(x, out_hbm, out, osem):
     outs = [pltpu.make_async_copy(out.at[k], out_hbm.at[k], osem.at[k]) for k in range(8)]
-    for copy in ins:
-        copy.start()
     upper = lax.broadcasted_iota(jnp.int32, (256, 256), 0) <= lax.broadcasted_iota(jnp.int32, (256, 256), 1)
     for k in range(8):
-        ins[k].wait()
         here = x[k]
         wide = here.astype(jnp.float32)
         turned = jnp.concatenate([wide[:, SPEC:], -wide[:, :SPEC]], axis=1).astype(jnp.bfloat16)
 
-        def product(left, lo, hi):
-            return lax.dot_general(
-                left[lo * 256 : lo * 256 + 256], here[hi * 256 : hi * 256 + 256], NT, preferred_element_type=jnp.float32
-            )
+        def product(imag, lo, hi):
+            left = (turned if imag else here)[lo * 256 : lo * 256 + 256]
+            return lax.dot_general(left, here[hi * 256 : hi * 256 + 256], NT, preferred_element_type=jnp.float32)
 
         for lo in range(2):
             for hi in range(2):
-                if lo < hi:
-                    block = product(here, lo, hi)
-                elif lo > hi:
-                    block = product(turned, lo, hi)
+                if lo != hi:
+                    block = product(int(lo > hi), lo, hi)
                 else:
-                    block = jnp.where(upper, product(here, lo, hi), product(turned, lo, hi))
-                out[k, lo * 256 : lo * 256 + 256, hi * 256 : hi * 256 + 256] = (block * (1.0 / SPEC)).astype(jnp.bfloat16)
+                    block = jnp.where(upper, product(0, lo, hi), product(1, lo, hi))
+                out[k, lo * 256 : lo * 256 + 256, hi * 256 : hi * 256 + 256] = block.astype(jnp.bfloat16)
         outs[k].start()
     for copy in outs:
         copy.wait()
@@ -277,49 +261,44 @@
     rows = NFFT // LANES
     frames = voltages.reshape(2, 2, FRAMES * rows, LANES).transpose(0, 2, 1, 3).reshape(2, FRAMES, 2 * rows, LANES)
     taps = filter_taps.reshape(2, 8, rows, LANES).transpose(0, 2, 1, 3).reshape(2 * rows * 8, LANES)
-    first, second = first_table(), second_table()
-    hbm = pl.BlockSpec(memory_space=pl.ANY)
+    tables = np.concatenate([second_table(), first_table()[None]], 0)
+    hbm, vmem = pl.BlockSpec(memory_space=pl.ANY), pl.BlockSpec(memory_space=pltpu.VMEM)
     dma = pltpu.SemaphoreType.DMA
     ordered = pl.pallas_call(
         channelize,
         name="channelize",
         out_shape=jax.ShapeDtypeStruct((8, 512, LANES), jnp.bfloat16),
-        in_specs=[hbm] * 4,
-        out_specs=hbm,
+        in_specs=[hbm, vmem, hbm],
+        out_specs=vmem,
         scratch_shapes=[
             pltpu.VMEM((2, FRAMES, 2 * rows, LANES), jnp.int32),
-            pltpu.VMEM(taps.shape, jnp.float32),
             pltpu.VMEM((3 * HALF, rows, LANES), jnp.float32),
-            pltpu.VMEM(first.shape, jnp.bfloat16),
-            pltpu.VMEM(second.shape, jnp.bfloat16),
+            pltpu.VMEM(tables.shape[1:], jnp.bfloat16),
+            pltpu.VMEM((R1,) + tables.shape[1:], jnp.bfloat16),
             pltpu.VMEM((SB, 2 * rows, LANES), jnp.bfloat16),
             pltpu.VMEM((SPEC * 64, LANES), jnp.float32),
             pltpu.VMEM((8 * C2, LANES), jnp.float32),
             pltpu.VMEM((512, 8, LANES), jnp.bfloat16),
             pltpu.VMEM((512, 8, LANES), jnp.bfloat16),
-            pltpu.VMEM((8, 512, LANES), jnp.bfloat16),
             dma((2, BLOCKS)),
-            dma((3,)),
-            dma((8,)),
+            dma((2,)),
             dma,
             dma((8,)),
-            pltpu.SemaphoreType.REGULAR,
+            pltpu.SemaphoreType.REGULAR((4,)),
         ],
-        compiler_params=pltpu.CompilerParams(collective_id=0, has_side_effects=True, vmem_limit_bytes=60 << 20),
-    )(frames, taps, jnp.asarray(first), jnp.asarray(second))
+        compiler_params=pltpu.CompilerParams(collective_id=0, has_side_effects=True, vmem_limit_bytes=52 << 20),
+    )(frames, taps, jnp.asarray(tables))
     return pl.pallas_call(
         correlate,
         name="correlate",
         out_shape=jax.ShapeDtypeStruct((8, 512, 512), jnp.bfloat16),
-        in_specs=[hbm],
+        in_specs=[vmem],
         out_specs=hbm,
         scratch_shapes=[
-            pltpu.VMEM((8, 512, LANES), jnp.bfloat16),
             pltpu.VMEM((8, 512, 512), jnp.bfloat16),
             dma((8,)),
-            dma((8,)),
         ],
-        compiler_params=pltpu.CompilerParams(vmem_limit_bytes=60 << 20),
+        compiler_params=pltpu.CompilerParams(vmem_limit_bytes=48 << 20),
     )(ordered)
 
 

time: 48.9 us -> 46.1 us (0.943)
  Pallas kernels: 48.8 us -> 45 us
  local copies, waits for them, and re-layouts: 0 us -> 0.95 us
    pallas_call x1, Pallas kernels: 5.1 us -> 2.7 us  [per_device(): pl.pallas_call(correlate, name='correlate', out_shape=jax.ShapeDtypeStruc...]
    pallas_call x1, Pallas kernels: 43.7 us -> 42.3 us  [per_device(): pl.pallas_call(channelize, name='channelize', out_shape=jax.ShapeDtypeStr...]
    unnamed x0 -> x2, local copies, waits for them, and re-layouts: none -> 0.95 us
where the time goes in v1:
time: 46.1 us; the launch traced here: 46 us
  Pallas kernels  45 us (98%)
  local copies, waits for them, and re-layouts  0.95 us (2%)
    pallas_call x1, Pallas kernels, per_device(): pl.pallas_call(channelize, name='channelize', out_shape=jax.ShapeDtypeStr...  42.3 us
    pallas_call x1, Pallas kernels, per_device(): pl.pallas_call(correlate, name='correlate', out_shape=jax.ShapeDtypeStruc...  2.7 us
    unnamed x2, local copies, waits for them, and re-layouts  0.95 us

profile of v1, /device:TPU:1, one launch (start us, length us, event | category | flops | bytes accessed | tf_op | source)
XLA Modules:
  0.0 46.0 jit_solution(12337550682177744409)
XLA Ops:
  0.0 0.0 copy-start
  0.0 0.9 %copy-done = f32[16,4096]{1,0:T(8,128)S(1)} copy-done((f32[16,4096]{1,0:T(8,128)S(1)}, f32[16,4096]{1,0:T(8,128)}, u32[]{:S(2)}) %copy-start) | copy-done | bytes 262168
  1.0 42.3 %channelize.1.x = bf16[8,512,128]{2,1,0:T(8,128)(2,1)S(1)} custom-call(s32[2,79,64,128]{3,2,1,0:T(8,128)} %bitcast.11, f32[512,128]{1,0:T(8,128)S(1)} %bitcast.10, bf16[33,128,256]{2,1,0:T(8,128)(2,1)} %constant.2.clone.t_hbm), custom_call_target="tpu_custom_call" | custom-call | tf_op jit(solution)/shard_map/channelize/pallas_call | solution.py:267
  43.3 2.7 %correlate.1 = bf16[8,512,512]{2,1,0:T(8,128)(2,1)} custom-call(bf16[8,512,128]{2,1,0:T(8,128)(2,1)S(1)} %channelize.1.x), custom_call_target="tpu_custom_call" | custom-call | tf_op jit(solution)/shard_map/correlate/pallas_call | solution.py:291
Async XLA Ops:
  0.0 0.9 %copy-start = (f32[16,4096]{1,0:T(8,128)S(1)}, f32[16,4096]{1,0:T(8,128)}, u32[]{:S(2)}) copy-start(f32[16,4096]{1,0:T(8,128)} %param.4) | copy-start | bytes 786436

commit v2 on v1

--- a/solution.py
+++ b/solution.py
@@ -56,6 +56,22 @@
     y_part = [high * 2, 2 - high * 2]
     c_part = [core, 1 - core]
     return chan, {(dz, dh, dc): z_part[dz] + (y_part[dh] + c_part[dc]) for dz in range(8) for dh in range(2) for dc in range(2)}
+
+
+def far_first():
+    def hops(to):
+        dz, dx, low, high, _ = to
+        return min(dz, 8 - dz) + min(dx, 4 - dx) + (1 if low else 2 * high)
+
+    every = [(dz, dx, low, high, dc) for dx in range(4) for low in range(2) for high in range(2) for dz in Z_ORDER for dc in range(2)]
+    every = sorted((to for to in every if any(to)), key=lambda to: -hops(to))
+    across, within = [to for to in every if to[0]], [to for to in every if not to[0]]
+    order = []
+    for i, to in enumerate(across):
+        order.append(to)
+        if i % 5 == 1 and within:
+            order.append(within.pop(0))
+    return order + within
 
 
 def signal(sem, chan, tile):
@@ -134,18 +150,17 @@
             for q in range(2):
                 af[pl.ds(pl.multiple_of((base + quad * 4 + 2 * q) * 64, 128), 128), :] = out[:, q * 128 : (q + 1) * 128]
 
-    def send_to(sig, turn, group, to_chan, half):
+    def send_to(sig, place, to_chan, to_tile):
         pltpu.make_async_remote_copy(
-            src_ref=msg.at[(sig * 4 + turn) * C2 + half + 2 * to_chan],
+            src_ref=msg.at[place + 2 * to_chan],
             dst_ref=got.at[sig * 256 + me],
             send_sem=send,
-            recv_sem=recv.at[sig * 4 + turn],
-            device_id={"chan": to_chan, "tile": half * 4 + group},
+            recv_sem=recv.at[sig],
+            device_id={"chan": to_chan, "tile": to_tile},
             device_id_type=MESH,
         ).start()
 
-    def group_step(sig, turn):
-        group = lax.rem(tile + turn, 4)
+    def transform(sig, group):
         for k in range(8):
             c1 = group * 8 + k
             real = af[pl.ds(c1, SPEC, stride=64), :]
@@ -156,23 +171,37 @@
             out = lax.dot_general(wbuf[c1], right, NT, preferred_element_type=jnp.float32)
             sbuf[k * C2 : (k + 1) * C2, :] = out[:C2] + out[C2:]
         for c2 in range(C2):
-            msg[(sig * 4 + turn) * C2 + c2] = sbuf[pl.ds(c2, 8, stride=C2), :].astype(jnp.bfloat16)
-        if sig == 0:
-
-            @pl.when(turn > 0)
-            def _():
-                pl.semaphore_wait(ready.at[turn], 1)
-
-        halves = [lax.div(tile, 4), 1 - lax.div(tile, 4)]
+            msg[(sig * 4 + group) * C2 + c2] = sbuf[pl.ds(c2, 8, stride=C2), :].astype(jnp.bfloat16)
+
+    def first_sends(turn, carry):
+        group = lax.rem(tile + turn, 4)
+        transform(0, group)
+
+        @pl.when(turn > 0)
+        def _():
+            pl.semaphore_wait(ready.at[turn], 1)
+
+        own_half = lax.div(tile, 4)
         for dx in range(2):
+            half = 1 - own_half if dx else own_half
             for dh in range(2):
                 for dz in Z_ORDER:
                     for dc in range(2):
-                        to = functools.partial(send_to, sig, turn, group, chan_at[dz, dh, dc], halves[dx])
+                        to = functools.partial(send_to, 0, group * C2 + half, chan_at[dz, dh, dc], half * 4 + group)
                         if dx or dh or dz or dc:
                             to()
                         else:
                             pl.when(turn != 0)(to)
+        return carry
+
+    def second_sends():
+        x, low = lax.div(tile, 2), lax.rem(tile, 2)
+        x_at = [lax.rem(x + dx, 4) for dx in range(4)]
+        low_at = [low, 1 - low]
+        tiles = {(dx, dl): x_at[dx] * 2 + low_at[dl] for dx in range(4) for dl in range(2)}
+        places = {to: (4 + lax.rem(at, 4)) * C2 + lax.div(at, 4) for to, at in tiles.items()}
+        for dz, dx, dl, dh, dc in far_first():
+            send_to(1, places[dx, dl], chan_at[dz, dh, dc], tiles[dx, dl])
 
     for sig in range(2):
 
@@ -187,8 +216,8 @@
             filter_block(sig, number)
             return carry
 
-        def send_step(turn, carry):
-            group_step(sig, turn)
+        def transform_step(group, carry):
+            transform(1, group)
             return carry
 
         if sig == 0:
@@ -201,34 +230,34 @@
             for turn in range(1, 4):
                 signal(ready.at[turn], chan, tile_at[8 - turn])
             second_in.wait()
-        lax.fori_loop(0, 4, send_step, 0)
-        got[sig * 256 + me] = msg[sig * 256 + 2 * chan + lax.div(tile, 4)]
+            lax.fori_loop(0, 4, first_sends, 0)
+        else:
+            lax.fori_loop(0, 4, transform_step, 0)
+            second_sends()
+        got[sig * 256 + me] = msg[(sig * 4 + lax.rem(tile, 4)) * C2 + 2 * chan + lax.div(tile, 4)]
 
     to = lax.broadcasted_iota(jnp.int32, (256, 256), 0)
     come = lax.broadcasted_iota(jnp.int32, (256, 256), 1)
     sort = (to == (come % 8) * 32 + (come // 8 % 16) * 2 + come // 128).astype(jnp.bfloat16)
 
-    for turn in range(4):
-        for sig in range(2):
-            count = pl.ds(0, 64 if turn else 63)
-            pltpu.make_async_copy(msg.at[count], got.at[count], recv.at[sig * 4 + turn]).wait()
-        group = lax.rem(tile + 4 - turn, 4)
-        for half in range(2):
-            from_tile = half * 4 + group
-            right = jnp.concatenate(
-                [
-                    jnp.concatenate(
-                        [got[pl.ds(sig * 256 + from_tile * 32 + 16 * q, 16)].reshape(128, LANES) for sig in range(2)], axis=0
-                    )
-                    for q in range(2)
-                ],
-                axis=1,
-            )
-            rows = jnp.dot(sort, right, preferred_element_type=jnp.float32)
-            for q in range(2):
-                here = pl.ds(pl.multiple_of(from_tile * 64 + 32 * q, 32), 32)
-                part = rows[:, q * 128 : (q + 1) * 128]
-                ordered[:, here, :] = part.astype(jnp.bfloat16).reshape(8, 32, LANES)
+    others = pl.ds(0, 255)
+    for sig in range(2):
+        pltpu.make_async_copy(msg.at[others], got.at[others], recv.at[sig]).wait()
+    for from_tile in range(8):
+        right = jnp.concatenate(
+            [
+                jnp.concatenate(
+                    [got[sig * 256 + from_tile * 32 + 16 * q : sig * 256 + from_tile * 32 + 16 * q + 16].reshape(128, LANES) for sig in range(2)], axis=0
+                )
+                for q in range(2)
+            ],
+            axis=1,
+        )
+        rows = jnp.dot(sort, right, preferred_element_type=jnp.float32)
+        for q in range(2):
+            here = slice(from_tile * 64 + 32 * q, from_tile * 64 + 32 * q + 32)
+            part = rows[:, q * 128 : (q + 1) * 128]
+            ordered[:, here, :] = part.astype(jnp.bfloat16).reshape(8, 32, LANES)
     everything = pl.ds(0, 510)
     pltpu.make_async_copy(msg.at[everything], got.at[everything], send).wait()
 
@@ -283,7 +312,7 @@
             dma((2, BLOCKS)),
             dma((2,)),
             dma,
-            dma((8,)),
+            dma((2,)),
             pltpu.SemaphoreType.REGULAR((4,)),
         ],
         compiler_params=pltpu.CompilerParams(collective_id=0, has_side_effects=True, vmem_limit_bytes=52 << 20),

time: 46.1 us -> 44.4 us (0.963)
  Pallas kernels: 45 us -> 43.3 us
    pallas_call x1, Pallas kernels: 42.3 us -> 40.6 us  [per_device(): pl.pallas_call(channelize, name='channelize', out_shape=jax.ShapeDtypeStr...]
where the time goes in v2:
time: 44.4 us; the launch traced here: 44.3 us
  Pallas kernels  43.3 us (98%)
  local copies, waits for them, and re-layouts  0.95 us (2%)
    pallas_call x1, Pallas kernels, per_device(): pl.pallas_call(channelize, name='channelize', out_shape=jax.ShapeDtypeStr...  40.6 us
    pallas_call x1, Pallas kernels, per_device(): pl.pallas_call(correlate, name='correlate', out_shape=jax.ShapeDtypeStruc...  2.7 us
    unnamed x2, local copies, waits for them, and re-layouts  0.95 us

profile of v2, /device:TPU:1, one launch (start us, length us, event | category | flops | bytes accessed | tf_op | source)
XLA Modules:
  0.0 44.3 jit_solution(17776317518615781211)
XLA Ops:
  0.0 0.0 copy-start
  0.0 0.9 %copy-done = f32[16,4096]{1,0:T(8,128)S(1)} copy-done((f32[16,4096]{1,0:T(8,128)S(1)}, f32[16,4096]{1,0:T(8,128)}, u32[]{:S(2)}) %copy-start) | copy-done | bytes 262168
  1.0 40.6 %channelize.1.x = bf16[8,512,128]{2,1,0:T(8,128)(2,1)S(1)} custom-call(s32[2,79,64,128]{3,2,1,0:T(8,128)} %bitcast.11, f32[512,128]{1,0:T(8,128)S(1)} %bitcast.10, bf16[33,128,256]{2,1,0:T(8,128)(2,1)} %constant.2.clone.t_hbm), custom_call_target="tpu_custom_call" | custom-call | tf_op jit(solution)/shard_map/channelize/pallas_call | solution.py:296
  41.6 2.7 %correlate.1 = bf16[8,512,512]{2,1,0:T(8,128)(2,1)} custom-call(bf16[8,512,128]{2,1,0:T(8,128)(2,1)S(1)} %channelize.1.x), custom_call_target="tpu_custom_call" | custom-call | tf_op jit(solution)/shard_map/correlate/pallas_call | solution.py:320
Async XLA Ops:
  0.0 0.9 %copy-start = (f32[16,4096]{1,0:T(8,128)S(1)}, f32[16,4096]{1,0:T(8,128)}, u32[]{:S(2)}) copy-start(f32[16,4096]{1,0:T(8,128)} %param.4) | copy-start | bytes 786436

commit v3 on v2

--- a/solution.py
+++ b/solution.py
@@ -94,10 +94,8 @@
     frames_in(0, 0).start()
     frames_in(1, 0).start()
     first_in.start()
-    for chunk in range(1, BLOCKS):
-        for part in range(2):
-            frames_in(part, chunk).start()
-    second_in.start()
+    frames_in(0, 1).start()
+    frames_in(1, 1).start()
 
     for dz in Z_ORDER:
         for dx in range(2):
@@ -137,18 +135,22 @@
         second = short(1, ahead - odd) + shared
         return jnp.stack([first, second], axis=1).reshape(SB, 8, LANES)
 
-    def filter_block(sig, number):
+    def first_stage(number, slot, quad):
+        pairs = [xs[slot, quad * 4 + 2 * q : quad * 4 + 2 * q + 2].reshape(128, LANES) for q in range(2)]
+        right = jnp.concatenate([jnp.concatenate([pair, pair], axis=0) for pair in pairs], axis=1)
+        out = jnp.dot(dbuf[...], right, preferred_element_type=jnp.float32)
+        for q in range(2):
+            where = pl.ds(pl.multiple_of((number * SB + quad * 4 + 2 * q) * 64, 128), 128)
+            af[where, :] = out[:, q * 128 : (q + 1) * 128]
+
+    def filter_block(sig, number, slot, before=None):
         base = number * SB
         for part in range(2):
             for pair in range(2):
+                if before is not None:
+                    first_stage(before, 1 - slot, part * 2 + pair)
                 both = jnp.concatenate([filter_rows(sig, part, 2 * pair + i, base) for i in range(2)], axis=1)
-                xs[:, part * 32 + pair * 16 : part * 32 + pair * 16 + 16, :] = both.astype(jnp.bfloat16)
-        for quad in range(SB // 4):
-            pairs = [xs[quad * 4 + 2 * q : quad * 4 + 2 * q + 2].reshape(128, LANES) for q in range(2)]
-            right = jnp.concatenate([jnp.concatenate([pair, pair], axis=0) for pair in pairs], axis=1)
-            out = jnp.dot(dbuf[...], right, preferred_element_type=jnp.float32)
-            for q in range(2):
-                af[pl.ds(pl.multiple_of((base + quad * 4 + 2 * q) * 64, 128), 128), :] = out[:, q * 128 : (q + 1) * 128]
+                xs[slot, :, part * 32 + pair * 16 : part * 32 + pair * 16 + 16, :] = both.astype(jnp.bfloat16)
 
     def send_to(sig, place, to_chan, to_tile):
         pltpu.make_async_remote_copy(
@@ -208,12 +210,10 @@
         def filter_step(number, carry):
             if sig == 0:
 
-                @pl.when(number > 0)
-                def _():
-                    frames_in(0, number).wait()
-                    frames_in(1, number).wait()
-
-            filter_block(sig, number)
+                frames_in(0, number).wait()
+                frames_in(1, number).wait()
+
+            filter_block(sig, number, lax.rem(number, 2), number - 1)
             return carry
 
         def transform_step(group, carry):
@@ -223,8 +223,15 @@
         if sig == 0:
             frames_in(0, 0).wait()
             frames_in(1, 0).wait()
+            for chunk in range(2, BLOCKS):
+                frames_in(0, chunk).start()
+                frames_in(1, chunk).start()
+            second_in.start()
             first_in.wait()
-        lax.fori_loop(0, BLOCKS, filter_step, 0)
+        filter_block(sig, 0, 0)
+        lax.fori_loop(1, BLOCKS, filter_step, 0)
+        for quad in range(SB // 4):
+            first_stage(BLOCKS - 1, (BLOCKS - 1) % 2, quad)
         if sig == 0:
             pl.semaphore_wait(barrier, 66)
             for turn in range(1, 4):
@@ -304,7 +311,7 @@
             pltpu.VMEM((3 * HALF, rows, LANES), jnp.float32),
             pltpu.VMEM(tables.shape[1:], jnp.bfloat16),
             pltpu.VMEM((R1,) + tables.shape[1:], jnp.bfloat16),
-            pltpu.VMEM((SB, 2 * rows, LANES), jnp.bfloat16),
+            pltpu.VMEM((2, SB, 2 * rows, LANES), jnp.bfloat16),
             pltpu.VMEM((SPEC * 64, LANES), jnp.float32),
             pltpu.VMEM((8 * C2, LANES), jnp.float32),
             pltpu.VMEM((512, 8, LANES), jnp.bfloat16),

time: 44.4 us -> 43.7 us (0.984)
  Pallas kernels: 43.3 us -> 42.6 us
    pallas_call x1, Pallas kernels: 40.6 us -> 39.9 us  [per_device(): pl.pallas_call(channelize, name='channelize', out_shape=jax.ShapeDtypeStr...]
where the time goes in v3:
time: 43.7 us; the launch traced here: 43.6 us
  Pallas kernels  42.6 us (97%)
  local copies, waits for them, and re-layouts  0.95 us (2%)
    pallas_call x1, Pallas kernels, per_device(): pl.pallas_call(channelize, name='channelize', out_shape=jax.ShapeDtypeStr...  39.9 us
    pallas_call x1, Pallas kernels, per_device(): pl.pallas_call(correlate, name='correlate', out_shape=jax.ShapeDtypeStruc...  2.7 us
    unnamed x2, local copies, waits for them, and re-layouts  0.95 us

profile of v3, /device:TPU:1, one launch (start us, length us, event | category | flops | bytes accessed | tf_op | source)
XLA Modules:
  0.0 43.6 jit_solution(14708086218953256796)
XLA Ops:
  0.0 0.0 copy-start
  0.0 0.9 %copy-done = f32[16,4096]{1,0:T(8,128)S(1)} copy-done((f32[16,4096]{1,0:T(8,128)S(1)}, f32[16,4096]{1,0:T(8,128)}, u32[]{:S(2)}) %copy-start) | copy-done | bytes 262168
  1.0 39.9 %channelize.1.x = bf16[8,512,128]{2,1,0:T(8,128)(2,1)S(1)} custom-call(s32[2,79,64,128]{3,2,1,0:T(8,128)} %bitcast.11, f32[512,128]{1,0:T(8,128)S(1)} %bitcast.10, bf16[33,128,256]{2,1,0:T(8,128)(2,1)} %constant.2.clone.t_hbm), custom_call_target="tpu_custom_call" | custom-call | tf_op jit(solution)/shard_map/channelize/pallas_call | solution.py:303
  40.9 2.7 %correlate.1 = bf16[8,512,512]{2,1,0:T(8,128)(2,1)} custom-call(bf16[8,512,128]{2,1,0:T(8,128)(2,1)S(1)} %channelize.1.x), custom_call_target="tpu_custom_call" | custom-call | tf_op jit(solution)/shard_map/correlate/pallas_call | solution.py:327
Async XLA Ops:
  0.0 0.9 %copy-start = (f32[16,4096]{1,0:T(8,128)S(1)}, f32[16,4096]{1,0:T(8,128)}, u32[]{:S(2)}) copy-start(f32[16,4096]{1,0:T(8,128)} %param.4) | copy-start | bytes 786436

commit v4 on v3

--- a/solution.py
+++ b/solution.py
@@ -143,21 +143,23 @@
             where = pl.ds(pl.multiple_of((number * SB + quad * 4 + 2 * q) * 64, 128), 128)
             af[where, :] = out[:, q * 128 : (q + 1) * 128]
 
-    def filter_block(sig, number, slot, before=None):
+    def filter_block(sig, number, slot, before=None, copies=()):
         base = number * SB
         for part in range(2):
+            if copies:
+                copies[part].wait()
             for pair in range(2):
                 if before is not None:
                     first_stage(before, 1 - slot, part * 2 + pair)
                 both = jnp.concatenate([filter_rows(sig, part, 2 * pair + i, base) for i in range(2)], axis=1)
                 xs[slot, :, part * 32 + pair * 16 : part * 32 + pair * 16 + 16, :] = both.astype(jnp.bfloat16)
 
-    def send_to(sig, place, to_chan, to_tile):
+    def send_to(sig, place, to_chan, to_tile, slot):
         pltpu.make_async_remote_copy(
             src_ref=msg.at[place + 2 * to_chan],
             dst_ref=got.at[sig * 256 + me],
             send_sem=send,
-            recv_sem=recv.at[sig],
+            recv_sem=recv.at[slot],
             device_id={"chan": to_chan, "tile": to_tile},
             device_id_type=MESH,
         ).start()
@@ -189,7 +191,7 @@
             for dh in range(2):
                 for dz in Z_ORDER:
                     for dc in range(2):
-                        to = functools.partial(send_to, 0, group * C2 + half, chan_at[dz, dh, dc], half * 4 + group)
+                        to = functools.partial(send_to, 0, group * C2 + half, chan_at[dz, dh, dc], half * 4 + group, 8)
                         if dx or dh or dz or dc:
                             to()
                         else:
@@ -203,7 +205,7 @@
         tiles = {(dx, dl): x_at[dx] * 2 + low_at[dl] for dx in range(4) for dl in range(2)}
         places = {to: (4 + lax.rem(at, 4)) * C2 + lax.div(at, 4) for to, at in tiles.items()}
         for dz, dx, dl, dh, dc in far_first():
-            send_to(1, places[dx, dl], chan_at[dz, dh, dc], tiles[dx, dl])
+            send_to(1, places[dx, dl], chan_at[dz, dh, dc], tiles[dx, dl], dx * 2 + dl)
 
     for sig in range(2):
 
@@ -221,14 +223,14 @@
             return carry
 
         if sig == 0:
-            frames_in(0, 0).wait()
-            frames_in(1, 0).wait()
+            filter_block(sig, 0, 0, copies=(frames_in(0, 0), frames_in(1, 0)))
             for chunk in range(2, BLOCKS):
                 frames_in(0, chunk).start()
                 frames_in(1, chunk).start()
             second_in.start()
             first_in.wait()
-        filter_block(sig, 0, 0)
+        else:
+            filter_block(sig, 0, 0)
         lax.fori_loop(1, BLOCKS, filter_step, 0)
         for quad in range(SB // 4):
             first_stage(BLOCKS - 1, (BLOCKS - 1) % 2, quad)
@@ -248,13 +250,16 @@
     sort = (to == (come % 8) * 32 + (come // 8 % 16) * 2 + come // 128).astype(jnp.bfloat16)
 
     others = pl.ds(0, 255)
-    for sig in range(2):
-        pltpu.make_async_copy(msg.at[others], got.at[others], recv.at[sig]).wait()
-    for from_tile in range(8):
+    pltpu.make_async_copy(msg.at[others], got.at[others], recv.at[8]).wait()
+    x, low = lax.div(tile, 2), lax.rem(tile, 2)
+    for dx, dl in ((2, 1), (2, 0), (1, 1), (3, 1), (1, 0), (3, 0), (0, 1), (0, 0)):
+        some = pl.ds(0, 32 if dx or dl else 31)
+        pltpu.make_async_copy(msg.at[some], got.at[some], recv.at[dx * 2 + dl]).wait()
+        from_tile = lax.rem(x + 4 - dx, 4) * 2 + (1 - low if dl else low)
         right = jnp.concatenate(
             [
                 jnp.concatenate(
-                    [got[sig * 256 + from_tile * 32 + 16 * q : sig * 256 + from_tile * 32 + 16 * q + 16].reshape(128, LANES) for sig in range(2)], axis=0
+                    [got[pl.ds(sig * 256 + from_tile * 32 + 16 * q, 16)].reshape(128, LANES) for sig in range(2)], axis=0
                 )
                 for q in range(2)
             ],
@@ -262,7 +267,7 @@
         )
         rows = jnp.dot(sort, right, preferred_element_type=jnp.float32)
         for q in range(2):
-            here = slice(from_tile * 64 + 32 * q, from_tile * 64 + 32 * q + 32)
+            here = pl.ds(pl.multiple_of(from_tile * 64 + 32 * q, 32), 32)
             part = rows[:, q * 128 : (q + 1) * 128]
             ordered[:, here, :] = part.astype(jnp.bfloat16).reshape(8, 32, LANES)
     everything = pl.ds(0, 510)
@@ -319,7 +324,7 @@
             dma((2, BLOCKS)),
             dma((2,)),
             dma,
-            dma((2,)),
+            dma((9,)),
             pltpu.SemaphoreType.REGULAR((4,)),
         ],
         compiler_params=pltpu.CompilerParams(collective_id=0, has_side_effects=True, vmem_limit_bytes=52 << 20),

time: 43.7 us -> 44.5 us (1.018)
  Pallas kernels: 42.6 us -> 43.5 us
    pallas_call x1, Pallas kernels: 39.9 us -> 40.8 us  [per_device(): pl.pallas_call(channelize, name='channelize', out_shape=jax.ShapeDtypeStr...]
where the time goes in v4:
time: 44.5 us; the launch traced here: 44.4 us
  Pallas kernels  43.5 us (98%)
  local copies, waits for them, and re-layouts  0.95 us (2%)
    pallas_call x1, Pallas kernels, per_device(): pl.pallas_call(channelize, name='channelize', out_shape=jax.ShapeDtypeStr...  40.8 us
    pallas_call x1, Pallas kernels, per_device(): pl.pallas_call(correlate, name='correlate', out_shape=jax.ShapeDtypeStruc...  2.7 us
    unnamed x2, local copies, waits for them, and re-layouts  0.95 us

profile of v4, /device:TPU:1, one launch (start us, length us, event | category | flops | bytes accessed | tf_op | source)
XLA Modules:
  0.0 44.4 jit_solution(6307940079076723597)
XLA Ops:
  0.0 0.0 copy-start
  0.0 0.9 %copy-done = f32[16,4096]{1,0:T(8,128)S(1)} copy-done((f32[16,4096]{1,0:T(8,128)S(1)}, f32[16,4096]{1,0:T(8,128)}, u32[]{:S(2)}) %copy-start) | copy-done | bytes 262168
  1.0 40.8 %channelize.1.x = bf16[8,512,128]{2,1,0:T(8,128)(2,1)S(1)} custom-call(s32[2,79,64,128]{3,2,1,0:T(8,128)} %bitcast.11, f32[512,128]{1,0:T(8,128)S(1)} %bitcast.10, bf16[33,128,256]{2,1,0:T(8,128)(2,1)} %constant.2.clone.t_hbm), custom_call_target="tpu_custom_call" | custom-call | tf_op jit(solution)/shard_map/channelize/pallas_call | solution.py:308
  41.7 2.7 %correlate.1 = bf16[8,512,512]{2,1,0:T(8,128)(2,1)} custom-call(bf16[8,512,128]{2,1,0:T(8,128)(2,1)S(1)} %channelize.1.x), custom_call_target="tpu_custom_call" | custom-call | tf_op jit(solution)/shard_map/correlate/pallas_call | solution.py:332
Async XLA Ops:
  0.0 0.9 %copy-start = (f32[16,4096]{1,0:T(8,128)S(1)}, f32[16,4096]{1,0:T(8,128)}, u32[]{:S(2)}) copy-start(f32[16,4096]{1,0:T(8,128)} %param.4) | copy-start | bytes 786436

commit v5 on v4

--- a/solution.py
+++ b/solution.py
@@ -143,11 +143,9 @@
             where = pl.ds(pl.multiple_of((number * SB + quad * 4 + 2 * q) * 64, 128), 128)
             af[where, :] = out[:, q * 128 : (q + 1) * 128]
 
-    def filter_block(sig, number, slot, before=None, copies=()):
+    def filter_block(sig, number, slot, before=None):
         base = number * SB
         for part in range(2):
-            if copies:
-                copies[part].wait()
             for pair in range(2):
                 if before is not None:
                     first_stage(before, 1 - slot, part * 2 + pair)
@@ -223,14 +221,14 @@
             return carry
 
         if sig == 0:
-            filter_block(sig, 0, 0, copies=(frames_in(0, 0), frames_in(1, 0)))
+            frames_in(0, 0).wait()
+            frames_in(1, 0).wait()
             for chunk in range(2, BLOCKS):
                 frames_in(0, chunk).start()
                 frames_in(1, chunk).start()
             second_in.start()
             first_in.wait()
-        else:
-            filter_block(sig, 0, 0)
+        filter_block(sig, 0, 0)
         lax.fori_loop(1, BLOCKS, filter_step, 0)
         for quad in range(SB // 4):
             first_stage(BLOCKS - 1, (BLOCKS - 1) % 2, quad)

time: 44.5 us -> 44.7 us (level)
  no operation moved by 1% of the time
where the time goes in v5:
time: 44.7 us; the launch traced here: 44.6 us
  Pallas kernels  43.6 us (98%)
  local copies, waits for them, and re-layouts  0.95 us (2%)
    pallas_call x1, Pallas kernels, per_device(): pl.pallas_call(channelize, name='channelize', out_shape=jax.ShapeDtypeStr...  40.9 us
    pallas_call x1, Pallas kernels, per_device(): pl.pallas_call(correlate, name='correlate', out_shape=jax.ShapeDtypeStruc...  2.7 us
    unnamed x2, local copies, waits for them, and re-layouts  0.95 us

profile of v5, /device:TPU:1, one launch (start us, length us, event | category | flops | bytes accessed | tf_op | source)
XLA Modules:
  0.0 44.6 jit_solution(13704990530389636239)
XLA Ops:
  0.0 0.0 copy-start
  0.0 0.9 %copy-done = f32[16,4096]{1,0:T(8,128)S(1)} copy-done((f32[16,4096]{1,0:T(8,128)S(1)}, f32[16,4096]{1,0:T(8,128)}, u32[]{:S(2)}) %copy-start) | copy-done | bytes 262168
  1.0 40.9 %channelize.1.x = bf16[8,512,128]{2,1,0:T(8,128)(2,1)S(1)} custom-call(s32[2,79,64,128]{3,2,1,0:T(8,128)} %bitcast.11, f32[512,128]{1,0:T(8,128)S(1)} %bitcast.10, bf16[33,128,256]{2,1,0:T(8,128)(2,1)} %constant.2.clone.t_hbm), custom_call_target="tpu_custom_call" | custom-call | tf_op jit(solution)/shard_map/channelize/pallas_call | solution.py:306
  41.9 2.7 %correlate.1 = bf16[8,512,512]{2,1,0:T(8,128)(2,1)} custom-call(bf16[8,512,128]{2,1,0:T(8,128)(2,1)S(1)} %channelize.1.x), custom_call_target="tpu_custom_call" | custom-call | tf_op jit(solution)/shard_map/correlate/pallas_call | solution.py:330
Async XLA Ops:
  0.0 0.9 %copy-start = (f32[16,4096]{1,0:T(8,128)S(1)}, f32[16,4096]{1,0:T(8,128)}, u32[]{:S(2)}) copy-start(f32[16,4096]{1,0:T(8,128)} %param.4) | copy-start | bytes 786436

commit v6 on v3

--- a/solution.py
+++ b/solution.py
@@ -90,7 +90,11 @@
         return pltpu.make_async_copy(v_hbm.at[part, where], vbuf.at[part, where], vsem.at[part, chunk])
 
     first_in = pltpu.make_async_copy(t_hbm.at[R1], dbuf, csem.at[0])
-    second_in = pltpu.make_async_copy(t_hbm.at[pl.ds(0, R1)], wbuf, csem.at[1])
+
+    def second_in(turn):
+        where = pl.ds(lax.rem(tile + turn, 4) * 8, 8)
+        return pltpu.make_async_copy(t_hbm.at[where], wbuf.at[where], csem.at[1 + turn])
+
     frames_in(0, 0).start()
     frames_in(1, 0).start()
     first_in.start()
@@ -177,6 +181,7 @@
 
     def first_sends(turn, carry):
         group = lax.rem(tile + turn, 4)
+        second_in(turn).wait()
         transform(0, group)
 
         @pl.when(turn > 0)
@@ -226,7 +231,10 @@
             for chunk in range(2, BLOCKS):
                 frames_in(0, chunk).start()
                 frames_in(1, chunk).start()
-            second_in.start()
+                if chunk == 2:
+                    second_in(0).start()
+            for turn in range(1, 4):
+                second_in(turn).start()
             first_in.wait()
         filter_block(sig, 0, 0)
         lax.fori_loop(1, BLOCKS, filter_step, 0)
@@ -236,7 +244,6 @@
             pl.semaphore_wait(barrier, 66)
             for turn in range(1, 4):
                 signal(ready.at[turn], chan, tile_at[8 - turn])
-            second_in.wait()
             lax.fori_loop(0, 4, first_sends, 0)
         else:
             lax.fori_loop(0, 4, transform_step, 0)
@@ -317,7 +324,7 @@
             pltpu.VMEM((512, 8, LANES), jnp.bfloat16),
             pltpu.VMEM((512, 8, LANES), jnp.bfloat16),
             dma((2, BLOCKS)),
-            dma((2,)),
+            dma((5,)),
             dma,
             dma((2,)),
             pltpu.SemaphoreType.REGULAR((4,)),

time: 43.7 us -> 43.7 us (level)
  no operation moved by 1% of the time
where the time goes in v6:
time: 43.7 us; the launch traced here: 43.6 us
  Pallas kernels  42.7 us (98%)
  local copies, waits for them, and re-layouts  0.95 us (2%)
    pallas_call x1, Pallas kernels, per_device(): pl.pallas_call(channelize, name='channelize', out_shape=jax.ShapeDtypeStr...  40 us
    pallas_call x1, Pallas kernels, per_device(): pl.pallas_call(correlate, name='correlate', out_shape=jax.ShapeDtypeStruc...  2.7 us
    unnamed x2, local copies, waits for them, and re-layouts  0.95 us

profile of v6, /device:TPU:1, one launch (start us, length us, event | category | flops | bytes accessed | tf_op | source)
XLA Modules:
  0.0 43.6 jit_solution(16569889436624760460)
XLA Ops:
  0.0 0.0 copy-start
  0.0 0.9 %copy-done = f32[16,4096]{1,0:T(8,128)S(1)} copy-done((f32[16,4096]{1,0:T(8,128)S(1)}, f32[16,4096]{1,0:T(8,128)}, u32[]{:S(2)}) %copy-start) | copy-done | bytes 262168
  1.0 40.0 %channelize.1.x = bf16[8,512,128]{2,1,0:T(8,128)(2,1)S(1)} custom-call(s32[2,79,64,128]{3,2,1,0:T(8,128)} %bitcast.11, f32[512,128]{1,0:T(8,128)S(1)} %bitcast.10, bf16[33,128,256]{2,1,0:T(8,128)(2,1)} %constant.2.clone.t_hbm), custom_call_target="tpu_custom_call" | custom-call | tf_op jit(solution)/shard_map/channelize/pallas_call | solution.py:310
  40.9 2.7 %correlate.1 = bf16[8,512,512]{2,1,0:T(8,128)(2,1)} custom-call(bf16[8,512,128]{2,1,0:T(8,128)(2,1)S(1)} %channelize.1.x), custom_call_target="tpu_custom_call" | custom-call | tf_op jit(solution)/shard_map/correlate/pallas_call | solution.py:334
Async XLA Ops:
  0.0 0.9 %copy-start = (f32[16,4096]{1,0:T(8,128)S(1)}, f32[16,4096]{1,0:T(8,128)}, u32[]{:S(2)}) copy-start(f32[16,4096]{1,0:T(8,128)} %param.4) | copy-start | bytes 786436
